TPU v7x, 128 devices: a whole 4x4x4 slice. The times are simulated.
128 devices in a mesh: tx: 8 (over y, core), ty: 16 (over z, x).
Axes of the slice: x: 4, y: 4, z: 4, core: 2. Of those that a mesh axis runs over, the one named last changes fastest.
Arguments:
- scenes: bfloat16 [256, 128, 384], P(('tx', 'ty')), may hold values from -6 to 6
- foot_tile: int32 [8192], P(('tx', 'ty')), may hold values from 0 to 127, as said below
- foot_offset: int32 [8192], P(('tx', 'ty')), may hold values from 0 to 126, as said below
- foot_count: int32 [8192], P(('tx', 'ty')), may hold values from 1 to 2, as said below
- row_weight: int32 [16384], P(('tx', 'ty')), may hold values from 1 to 8
- stem_weight: bfloat16 [54, 128], replicated, may hold values from -0.875 to 0.875
- stem_bias: float32 [128], replicated, may hold values from -3 to 3
- first_weight: bfloat16 [1152, 256], replicated, may hold values from -0.1875 to 0.1875
- first_scale: float32 [256], replicated, may hold values from 0.5 to 1.5
- first_shift: float32 [256], replicated, may hold values from -2 to 2
- second_weight: bfloat16 [2304, 256], replicated, may hold values from -0.125 to 0.125
- second_scale: float32 [256], replicated, may hold values from 0.5 to 1.5
- second_shift: float32 [256], replicated, may hold values from -2 to 2
Outputs:
- encoded: bfloat16 [1024, 512, 256], P('tx', 'ty')
Inputs may be any that keep to these rules, and one draw needn't show every extreme that they name: `foot_tile`: the 64 entries of one device name different tiles; in every draw one tile is named by the first entry of every device. A program may carry tile numbers in any encoding that loses none of them, several to a word included. `foot_offset`: A program may carry offsets in any encoding that loses none of them, several to a word included. `foot_count`: the first entry of every device covers 2 rows. A program may carry counts in any encoding that loses none of them, several to a word included. `row_weight`: A program may carry the weights in any encoding that loses none of them, several to a word included.
All inputs are finite; a program needn't handle non-finite values.
Results may differ from a plain program's by a relative error of at most 0.0053.
Values may be sent and summed in bfloat16 or wider, within the bound.
A program may use at most 128 MiB of HBM per device.

v0:
```python
import jax
import jax.numpy as jnp
from jax import lax
from jax.sharding import PartitionSpec as P

TR = 128
TW = 32


def padded_2(x, sides, width):
    for axis, dim in sides:
        size, length = (lax.axis_size(axis), x.shape[dim])
        up = [(i, (i + 1) % size) for i in range(size - 1)]
        down = [(j, i) for i, j in up]
        last = lax.slice_in_dim(x, length - width, length, axis=dim)
        leading = lax.slice_in_dim(x, 0, width, axis=dim)
        before = lax.ppermute(last, axis, up)
        after = lax.ppermute(leading, axis, down)
        x = jnp.concatenate([before, x, after], axis=dim)
    return x


def make_strips(scene_block):
    scene_count, height, row_span = scene_block.shape
    padded = jnp.pad(scene_block, ((0, 0), (1, 0), (0, 0)))
    row_pairs = padded[:, :height].reshape(scene_count, height // 2, 2, row_span)
    third_rows = padded[:, 2::2]
    strips = jnp.concatenate([row_pairs, third_rows[:, :, None, :]], axis=2)
    return strips.reshape(scene_count * (height // 2), 3 * row_span)


def stem_rows(strips, stem_weight, stem_bias):
    count_rows = strips.shape[0]
    band_count = stem_weight.shape[0] // 9
    width_in = strips.shape[1] // (3 * band_count)
    width_out = width_in // 2
    pixels = strips.reshape(count_rows, 3, width_in, band_count)
    padded = jnp.pad(pixels, ((0, 0), (0, 0), (1, 0), (0, 0)))
    columns = [padded[:, :, offset : offset + 2 * width_out : 2, :] for offset in range(3)]
    tap_stack = jnp.stack(columns, axis=2)
    patches = tap_stack.transpose(0, 3, 1, 2, 4).reshape(count_rows * width_out, 9 * band_count)
    summed = jnp.dot(patches, stem_weight, preferred_element_type=jnp.float32) + stem_bias
    activated = jnp.maximum(summed, 0.0).astype(jnp.bfloat16)
    return activated.reshape(count_rows, width_out * stem_weight.shape[1])


def conv_layer(padded, weight, scale, shift, rows_out, cols_out):
    channels_in = padded.shape[2]
    channels_out = weight.shape[1]
    kernel = weight.reshape(3, 3, channels_in, channels_out)
    summed = jnp.zeros((rows_out * cols_out, channels_out), jnp.float32)
    for shift_row in range(3):
        for shift_col in range(3):
            window = padded[shift_row : shift_row + rows_out, shift_col : shift_col + cols_out]
            window = window.reshape(rows_out * cols_out, channels_in)
            summed = summed + jnp.dot(
                window, kernel[shift_row, shift_col], preferred_element_type=jnp.float32
            )
    activated = jnp.maximum(summed * scale + shift, 0.0)
    return activated.reshape(rows_out, cols_out, channels_out)


def per_device(
    scenes,
    foot_tile,
    foot_offset,
    foot_count,
    row_weight,
    stem_weight,
    stem_bias,
    first_weight,
    first_scale,
    first_shift,
    second_weight,
    second_scale,
    second_shift,
):
    devices = lax.axis_size("tx") * lax.axis_size("ty")
    my_tile = lax.axis_index("tx") * lax.axis_size("ty") + lax.axis_index("ty")
    entries = foot_tile.shape[0]
    rows_dev = row_weight.shape[0]
    capacity = rows_dev // entries
    channels = stem_weight.shape[1]
    all_tiles, all_offsets, all_counts, all_weights = (
        lax.all_gather(foot_tile, ("tx", "ty"), axis=0, tiled=True),
        lax.all_gather(foot_offset, ("tx", "ty"), axis=0, tiled=True),
        lax.all_gather(foot_count, ("tx", "ty"), axis=0, tiled=True),
        lax.all_gather(row_weight, ("tx", "ty"), axis=0, tiled=True),
    )
    tile_ids = jnp.arange(devices, dtype=jnp.int32)
    matches = foot_tile[None, :] == tile_ids[:, None]
    entry_pick = jnp.sum(
        jnp.where(matches, jnp.arange(entries, dtype=jnp.int32)[None, :], 0), axis=1
    )
    present = jnp.any(matches, axis=1).astype(jnp.bfloat16)
    strips = make_strips(scenes)
    features = stem_rows(strips, stem_weight, stem_bias)
    grouped = features.reshape(entries, capacity, features.shape[1])
    outgoing = jnp.take(grouped, entry_pick, axis=0) * present[:, None, None]
    arrived = lax.all_to_all(outgoing, ("tx", "ty"), split_axis=0, concat_axis=0, tiled=True)
    arrived = arrived.reshape(devices * capacity, TW * channels)
    aimed_here = (all_tiles.reshape(devices, entries) == my_tile).astype(jnp.int32)
    offsets = jnp.sum(aimed_here * all_offsets.reshape(devices, entries), axis=1)
    counts = jnp.sum(aimed_here * all_counts.reshape(devices, entries), axis=1)
    weights = jnp.sum(
        aimed_here[:, :, None] * all_weights.reshape(devices, entries, capacity), axis=1
    )
    slot_pos = jnp.arange(capacity, dtype=jnp.int32)
    usable = slot_pos[None, :] < counts[:, None]
    target_row = (offsets[:, None] + slot_pos[None, :]).reshape(devices * capacity)
    weight_used = jnp.where(usable, weights, 0).astype(jnp.float32).reshape(devices * capacity)
    blend_matrix = jnp.where(
        jnp.arange(TR, dtype=jnp.int32)[:, None] == target_row[None, :], weight_used[None, :], 0.0
    )
    numerator = jnp.dot(
        blend_matrix.astype(jnp.bfloat16), arrived, preferred_element_type=jnp.float32
    )
    denominator = jnp.sum(blend_matrix, axis=1)
    blended = (numerator / jnp.maximum(denominator, 1.0)[:, None]).astype(jnp.bfloat16)
    blended = blended.reshape(TR, TW, channels)
    extended = padded_2(blended, (("tx", 0), ("ty", 1)), 1)
    hidden = conv_layer(extended, first_weight, first_scale, first_shift, TR, TW).astype(
        jnp.bfloat16
    )
    hidden_wide = padded_2(hidden, (("tx", 0), ("ty", 1)), 1)
    second = conv_layer(hidden_wide, second_weight, second_scale, second_shift, TR, TW)
    return second.astype(jnp.bfloat16)


def solution(mesh):
    in_specs = (
        P(("tx", "ty"), None, None),
        P(("tx", "ty")),
        P(("tx", "ty")),
        P(("tx", "ty")),
        P(("tx", "ty")),
        P(),
        P(),
        P(),
        P(),
        P(),
        P(),
        P(),
        P(),
    )
    out_specs = P("tx", "ty", None)
    return jax.shard_map(
        per_device, mesh=mesh, in_specs=in_specs, out_specs=out_specs, check_vma=False
    )
```

profile of v0, /device:TPU:1, one launch (start us, length us, event | category | flops | bytes accessed | tf_op | source)
XLA Modules:
  0.0 276.0 jit_solution(11130161784171446283)
XLA Ops:
  6.5 0.8 select_reduce_fusion.1
  7.3 0.7 fusion.30
  8.1 1.0 pad_slice_fusion.8
  9.0 1.0 pad.8
  10.5 10.2 %concatenate.48 = bf16[128,2,64,6]{3,2,1,0:T(8,128)(2,1)} reshape(bf16[2,128,384]{2,1,0:T(8,128)(2,1)S(1)} %pad_slice_fusion.8) | data formatting | bytes 393216 | tf_op jit(solution)/shard_map/concatenate | solution.py:28
  20.7 6.2 %copy.34 = bf16[128,2,64,6]{0,2,3,1:T(8,128)(2,1)S(1)} copy(bf16[128,2,64,6]{3,2,1,0:T(8,128)(2,1)} %concatenate.48) | data formatting | bytes 393216 | tf_op jit(solution)/shard_map/concatenate | solution.py:28
  27.4 0.2 slice.173
  27.7 0.9 copy.39
  28.6 1.9 reshape.167
  30.6 0.5 fusion.13
  31.1 0.3 reshape_reshape.7
  31.4 7.6 %gather_fusion = bf16[128,2,4096]{2,1,0:T(2,128)(2,1)S(1)} fusion(bf16[64,2,4096]{2,1,0:T(2,128)(2,1)S(1)} %reshape_reshape.7, s32[1024]{0:T(1024)S(1)} %pad_clamp_fusion), kind=kCustom, calls=%fused_computation | custom fusion | bytes 4194816 | tf_op jit(solution)/shard_map/jit(_take)/gather | solution.py:99
  38.9 3.7 %fusion.14 = bf16[128,2,4096]{2,1,0:T(2,128)(2,1)} fusion(bf16[128,2,4096]{2,1,0:T(2,128)(2,1)S(1)} %gather_fusion, pred[128]{0:T(512)(128)(4,1)S(1)} %compare_and_fusion, bf16[128]{0:T(256)(128)(2,1)S(1)} %convert_element_type.59), kind=kLoop, calls=%fused_computation.35 | loop fusion | flops 2097152 | bytes 4194688 | tf_op jit(solution)/shard_map/mul | solution.py:99
  42.7 11.5 %all-to-all-start = ((bf16[128,2,4096]{2,1,0:T(2,128)(2,1)}), bf16[128,2,4096]{2,1,0:T(2,128)(2,1)S(1)}, u32[]{:S(2)}, u32[]{:S(2)}) async-start(bf16[128,2,4096]{2,1,0:T(2,128)(2,1)} %fusion.14), calls=%async_computation | async-start | bytes 4194304 | tf_op jit(solution)/shard_map/all_to_all | solution.py:100
  54.3 0.3 dynamic-update-slice
  54.5 0.3 dynamic-update-slice.2
  54.8 0.3 dynamic-update-slice.1
  55.1 0.3 copy-done.6
  55.4 0.3 copy-done.4
  55.8 61.8 %all-gather = s32[128,1,128]{2,1,0:T(1,128)S(1)} all-gather(s32[1,1,128]{2,1,0:T(1,128)S(1)} %bitcast.171), channel_id=1, replica_groups=mesh['tx'=8,'ty'=16] {'tx','ty'}, dimensions={0}, use_global_device_ids=true | all-gather | bytes 66048 | tf_op jit(solution)/shard_map/all_gather | solution.py:88
  117.7 88.7 %all-reduce.8.cloned.1.call-done = (s32[8192]{0:T(1024)}, s32[8192]{0:T(1024)}, s32[8192]{0:T(1024)}) async-done(((s32[8192]{0:T(1024)}, s32[8192]{0:T(1024)}, s32[8192]{0:T(1024)}), (s32[8192]{0:T(1024)}, s32[8192]{0:T(1024)}, s32[8192]{0:T(1024)})) %all-reduce.8.cloned.1.call-update) | async-done | bytes 98320
  206.4 0.8 broadcast_select_fusion.2
  207.3 0.8 broadcast_select_fusion.1
  209.2 2.2 reshape.168
  211.4 2.0 fusion.12
  213.6 3.6 %collective-permute-start = (bf16[1,32,128]{2,1,0:T(8,128)(2,1)S(1)}, bf16[1,32,128]{2,1,0:T(8,128)(2,1)S(1)}, u32[]{:S(2)}, u32[]{:S(2)}) collective-permute-start(bf16[1,32,128]{2,1,0:T(8,128)(2,1)S(1)} %bitcast.170), channel_id=1, source_target_pairs={{0,16},{16,32},{32,48},{48,64},{64,80},{80,96},{96,112},{1,17},{17... | collective-permute-start | bytes 24584 | tf_op jit(solution)/shard_map/ppermute | solution.py:17
  217.2 0.5 reshape_reshape.8
  217.7 1.9 collective-permute-start.1
  219.6 0.2 copy.40
  219.9 2.8 %collective-permute-done.1 = bf16[1,32,128]{2,1,0:T(8,128)(2,1)S(1)} collective-permute-done((bf16[1,32,128]{2,1,0:T(8,128)(2,1)S(1)}, bf16[1,32,128]{2,1,0:T(8,128)(2,1)S(1)}, u32[]{:S(2)}, u32[]{:S(2)}) %collective-permute-start.1) | collective-permute-done | bytes 8224 | tf_op jit(solution)/shard_map/ppermute | solution.py:18
  222.7 0.5 pad_maximum_fusion.6
  223.3 1.7 collective-permute-start.2
  225.0 1.3 collective-permute-start.3
  226.3 0.7 fusion.25
  227.0 0.7 fusion.26
  227.7 2.3 collective-permute-done.3
  230.0 3.4 %pad_maximum_fusion.5 = (bf16[128,32,128]{2,1,0:T(8,128)(2,1)S(1)}, bf16[128,32,128]{2,1,0:T(8,128)(2,1)S(1)}, bf16[128,32,128]{2,1,0:T(8,128)(2,1)S(1)}, bf16[1...) fusion(bf16[130,32,128]{2,1,0:T(8,128)(2,1)S(1)} %constant_dynamic-update-slice_, ...), kind=kLoop, calls=%fused_computation.50 | loop fusion | flops 12582912 | bytes 7422976 | tf_op jit(solution)/shard_map/concatenate | solution.py:19
  233.5 0.7 fusion.24
  234.1 0.7 convolution_add_fusion.12
  234.8 0.7 convolution_add_fusion.11
  235.5 0.7 convolution_add_fusion.10
  236.3 0.7 convolution_add_fusion.9
  237.0 0.7 convolution_add_fusion.8
  237.7 1.2 fusion.10
  239.0 3.7 %collective-permute-start.4 = (bf16[1,32,256]{2,1,0:T(8,128)(2,1)S(1)}, bf16[1,32,256]{2,1,0:T(8,128)(2,1)S(1)}, u32[]{:S(2)}, u32[]{:S(2)}) collective-permute-start(bf16[1,32,256]{2,1,0:T(8,128)(2,1)S(1)} %get-tuple-element.24), channel_id=1, source_target_pairs={{0,16},{16,32},{32,48},{48,64},{64,80},{80,96},{96,112},{1,17},{17... | collective-permute-start | bytes 49160 | tf_op jit(solution)/shard_map/ppermute | solution.py:17
  242.6 1.9 collective-permute-start.5
  244.6 3.1 %collective-permute-done.5 = bf16[1,32,256]{2,1,0:T(8,128)(2,1)S(1)} collective-permute-done((bf16[1,32,256]{2,1,0:T(8,128)(2,1)S(1)}, bf16[1,32,256]{2,1,0:T(8,128)(2,1)S(1)}, u32[]{:S(2)}, u32[]{:S(2)}) %collective-permute-start.5) | collective-permute-done | bytes 16416 | tf_op jit(solution)/shard_map/ppermute | solution.py:18
  247.7 0.2 pad_maximum_fusion.9
  247.9 2.6 collective-permute-start.6
  250.5 1.5 collective-permute-start.7
  252.0 0.3 pad_maximum_fusion.1
  252.3 1.6 fusion.23
  253.9 2.5 collective-permute-done.7
  256.4 1.8 maximum_maximum_fusion
  258.3 0.8 fusion.34
  259.1 1.6 fusion.35
  260.7 1.7 convolution_add_fusion.6
  262.4 0.7 convolution_add_fusion.5
  263.1 0.7 convolution_add_fusion.4
  263.8 0.7 convolution_add_fusion.3
  264.6 0.7 fusion.22
  265.3 0.7 convolution_add_fusion.2
  266.0 0.8 convolution_add_fusion.1
  266.8 2.4 fusion.9
  (73 shorter events, 2.6 us)
Async XLA Ops:
  6.5 24.0 %copy-start = (bf16[54,128]{1,0:T(8,128)(2,1)S(1)}, bf16[54,128]{1,0:T(8,128)(2,1)}, u32[]{:S(2)}) copy-start(bf16[54,128]{1,0:T(8,128)(2,1)} %param.18) | copy-start | bytes 41476
  27.7 2.9 %copy-start.12 = (f32[128]{0:T(128)S(1)}, f32[128]{0:T(128)}, u32[]{:S(2)}) copy-start(f32[128]{0:T(128)} %param.19) | copy-start | bytes 1540
  42.6 11.6 %copy-start.13 = (s32[64]{0:T(128)S(1)}, s32[64]{0:T(128)}, u32[]{:S(2)}) copy-start(s32[64]{0:T(128)} %param.14) | copy-start | bytes 772
  42.6 11.9 %copy-start.14 = (s32[64]{0:T(128)S(1)}, s32[64]{0:T(128)}, u32[]{:S(2)}) copy-start(s32[64]{0:T(128)} %param.16) | copy-start | bytes 772
  42.7 12.2 %copy-start.15 = (s32[64]{0:T(128)S(1)}, s32[64]{0:T(128)}, u32[]{:S(2)}) copy-start(s32[64]{0:T(128)} %param.15) | copy-start | bytes 772
  42.7 13.1 %copy-start.11 = (s32[128]{0:T(128)S(1)}, s32[128]{0:T(128)}, u32[]{:S(2)}) copy-start(s32[128]{0:T(128)} %param.17) | copy-start | bytes 1540
  42.7 166.5 %all-to-all-start = ((bf16[128,2,4096]{2,1,0:T(2,128)(2,1)}), bf16[128,2,4096]{2,1,0:T(2,128)(2,1)S(1)}, u32[]{:S(2)}, u32[]{:S(2)}) async-start(bf16[128,2,4096]{2,1,0:T(2,128)(2,1)} %fusion.14), calls=%async_computation | async-start | bytes 4194304 | tf_op jit(solution)/shard_map/all_to_all | solution.py:100
  54.2 152.2 %all-reduce.8.cloned.1.call-start = ((), (), s32[]{:S(2)}) async-start(), calls=%async_computation.1 | async-start | bytes 196608
  54.5 0.6 copy-start.5
  54.8 0.6 copy-start.6
  55.1 0.6 copy-start.4
  213.6 6.3 %collective-permute-start = (bf16[1,32,128]{2,1,0:T(8,128)(2,1)S(1)}, bf16[1,32,128]{2,1,0:T(8,128)(2,1)S(1)}, u32[]{:S(2)}, u32[]{:S(2)}) collective-permute-start(bf16[1,32,128]{2,1,0:T(8,128)(2,1)S(1)} %bitcast.170), channel_id=1, source_target_pairs={{0,16},{16,32},{32,48},{48,64},{64,80},{80,96},{96,112},{1,17},{17... | collective-permute-start | bytes 24584 | tf_op jit(solution)/shard_map/ppermute | solution.py:17
  217.7 5.0 %collective-permute-start.1 = (bf16[1,32,128]{2,1,0:T(8,128)(2,1)S(1)}, bf16[1,32,128]{2,1,0:T(8,128)(2,1)S(1)}, u32[]{:S(2)}, u32[]{:S(2)}) collective-permute-start(bf16[1,32,128]{2,1,0:T(8,128)(2,1)S(1)} %bitcast.169), channel_id=1, source_target_pairs={{16,0},{32,16},{48,32},{64,48},{80,64},{96,80},{112,96},{17,1},{33... | collective-permute-start | bytes 24584 | tf_op jit(solution)/shard_map/ppermute | solution.py:18
  222.7 3.7 %copy-start.3 = (bf16[1152,256]{1,0:T(8,128)(2,1)S(1)}, bf16[1152,256]{1,0:T(8,128)(2,1)}, u32[]{:S(2)}) copy-start(bf16[1152,256]{1,0:T(8,128)(2,1)} %param.20) | copy-start | bytes 1769476
  223.3 4.4 %collective-permute-start.2 = (bf16[130,1,128]{2,1,0:T(2,128)(2,1)S(1)}, bf16[130,1,128]{2,1,0:T(2,128)(2,1)S(1)}, u32[]{:S(2)}, u32[]{:S(2)}) collective-permute-start(bf16[130,1,128]{2,1,0:T(2,128)(2,1)S(1)} %get-tuple-element.35), channel_id=1, source_target_pairs={{0,1},{1,2},{2,3},{3,4},{4,5},{5,6},{6,7},{7,8},{8,9},{9,10},{10,1... | collective-permute-start | bytes 99848 | tf_op jit(solution)/shard_map/ppermute | solution.py:17
  225.0 5.0 %collective-permute-start.3 = (bf16[130,1,128]{2,1,0:T(2,128)(2,1)S(1)}, bf16[130,1,128]{2,1,0:T(2,128)(2,1)S(1)}, u32[]{:S(2)}, u32[]{:S(2)}) collective-permute-start(bf16[130,1,128]{2,1,0:T(2,128)(2,1)S(1)} %get-tuple-element.36), channel_id=1, source_target_pairs={{1,0},{2,1},{3,2},{4,3},{5,4},{6,5},{7,6},{8,7},{9,8},{10,9},{11,1... | collective-permute-start | bytes 99848 | tf_op jit(solution)/shard_map/ppermute | solution.py:18
  237.0 0.7 copy-start.7
  237.0 0.7 copy-start.8
  239.0 5.6 %collective-permute-start.4 = (bf16[1,32,256]{2,1,0:T(8,128)(2,1)S(1)}, bf16[1,32,256]{2,1,0:T(8,128)(2,1)S(1)}, u32[]{:S(2)}, u32[]{:S(2)}) collective-permute-start(bf16[1,32,256]{2,1,0:T(8,128)(2,1)S(1)} %get-tuple-element.24), channel_id=1, source_target_pairs={{0,16},{16,32},{32,48},{48,64},{64,80},{80,96},{96,112},{1,17},{17... | collective-permute-start | bytes 49160 | tf_op jit(solution)/shard_map/ppermute | solution.py:17
  242.6 5.1 %collective-permute-start.5 = (bf16[1,32,256]{2,1,0:T(8,128)(2,1)S(1)}, bf16[1,32,256]{2,1,0:T(8,128)(2,1)S(1)}, u32[]{:S(2)}, u32[]{:S(2)}) collective-permute-start(bf16[1,32,256]{2,1,0:T(8,128)(2,1)S(1)} %get-tuple-element.25), channel_id=1, source_target_pairs={{16,0},{32,16},{48,32},{64,48},{80,64},{96,80},{112,96},{17,1},{33... | collective-permute-start | bytes 49160 | tf_op jit(solution)/shard_map/ppermute | solution.py:18
  247.9 6.0 %collective-permute-start.6 = (bf16[130,1,256]{2,1,0:T(2,128)(2,1)S(1)}, bf16[130,1,256]{2,1,0:T(2,128)(2,1)S(1)}, u32[]{:S(2)}, u32[]{:S(2)}) collective-permute-start(bf16[130,1,256]{2,1,0:T(2,128)(2,1)S(1)} %get-tuple-element.20), channel_id=1, source_target_pairs={{0,1},{1,2},{2,3},{3,4},{4,5},{5,6},{6,7},{7,8},{8,9},{9,10},{10,1... | collective-permute-start | bytes 199688 | tf_op jit(solution)/shard_map/ppermute | solution.py:17
  250.5 5.9 %collective-permute-start.7 = (bf16[130,1,256]{2,1,0:T(2,128)(2,1)S(1)}, bf16[130,1,256]{2,1,0:T(2,128)(2,1)S(1)}, u32[]{:S(2)}, u32[]{:S(2)}) collective-permute-start(bf16[130,1,256]{2,1,0:T(2,128)(2,1)S(1)} %get-tuple-element.21), channel_id=1, source_target_pairs={{1,0},{2,1},{3,2},{4,3},{5,4},{6,5},{7,6},{8,7},{9,8},{10,9},{11,1... | collective-permute-start | bytes 199688 | tf_op jit(solution)/shard_map/ppermute | solution.py:18
  260.6 1.7 copy-start.2
  266.0 0.8 copy-start.9
  266.0 0.8 copy-start.10
  266.8 2.4 copy-start.1
Sparse Core Ops, SparseCore 0:
  60.3 146.0 all-reduce.7
where the time goes:
time: 280 us; the launch traced here: 276 us
  waiting for transfers between devices  99.4 us (36%)
  blocking collectives  61.8 us (22%)
  local copies, waits for them, and re-layouts  37.9 us (14%)
  starting transfers between devices  29.7 us (11%)
  matrix products  19.3 us (7%)
  between operations  14.1 us (5%)
  other arithmetic  13.7 us (5%)
    unnamed x2, waiting for transfers between devices  88.7 us
    all_gather x1, blocking collectives, per_device(): lax.all_gather(row_weight, ('tx', 'ty'), axis=0, tiled=True)  61.8 us
    dot_general x18, matrix products, conv_layer(): jnp.dot(window, kernel[shift_row, shift_col], preferred_element_type=jnp....  16.8 us
    concatenate x4, local copies, waits for them, and re-layouts, make_strips(): strips = jnp.concatenate([row_pairs, third_rows[:, :, None, :]], axis=2)  16.6 us
    ppermute x4, starting transfers between devices, padded_2(): before = lax.ppermute(last, axis, up)  11.6 us
    all_to_all x1, starting transfers between devices, per_device(): lax.all_to_all(outgoing, ('tx', 'ty'), split_axis=0, concat_axis=0, tiled...  11.5 us
    ppermute x4, waiting for transfers between devices, padded_2(): after = lax.ppermute(leading, axis, down)  10.7 us
    gather x1, local copies, waits for them, and re-layouts, per_device(): outgoing = jnp.take(grouped, entry_pick, axis=0) * present[:, None, None]  7.56 us
  transfers between devices with their start and end apart: 10, of which 5 were waited for; matrix products, arithmetic and copies ran while one was open for 3% of the time, Pallas kernels for 0%

commit v1 on v0

v1 whole, which is shorter than its diff:
```python
import jax
import jax.numpy as jnp
from jax import lax
from jax.experimental import pallas as pl
from jax.experimental.pallas import tpu as pltpu
from jax.sharding import PartitionSpec as P

TR, TW = 128, 32
NX, NY = 8, 16
DEV = NX * NY
ENT = 64
C1, C2 = 128, 256
PITCH1 = 152
PITCH2 = 40
MB = 32
BF, F32 = jnp.bfloat16, jnp.float32
MESH = pl.DeviceIdType.MESH


def iota(shape, dim):
    return lax.broadcasted_iota(jnp.int32, shape, dim)


def pack_messages(scene, tile, offset, count, rweight, s32, o32, out):
    for c in range(3):
        s32[c, 0:8] = jnp.zeros((8, 128), F32)
        s32[c, 8:264] = scene[:, 128 * c : 128 * c + 128].astype(F32)
    first_row = (iota((ENT, 128), 0) % (ENT // 2)) != 0
    chunks = []
    for p in range(5):
        for c in range(3):
            rows = s32[c, pl.ds(7 + p, ENT, stride=4), :]
            if p == 0:
                rows = jnp.where(first_row, rows, 0.0)
            chunks.append(rows.astype(BF))
    pixels = jnp.concatenate(chunks, axis=1)
    onehot = (iota((DEV, ENT), 0) == tile[...]).astype(F32).astype(BF)
    picked = jnp.dot(onehot, pixels, preferred_element_type=F32)
    for r in range(15):
        o32[pl.ds(r, DEV, stride=16), :] = picked[:, 128 * r : 128 * r + 128]
    both = jnp.broadcast_to(rweight[...].astype(F32), (16, 128)).astype(BF)
    src, dst = iota((128, ENT), 0), iota((128, ENT), 1)
    w0 = jnp.dot(both, (src == 2 * dst).astype(F32).astype(BF), preferred_element_type=F32)[0:1]
    w1 = jnp.dot(both, (src == 2 * dst + 1).astype(F32).astype(BF), preferred_element_type=F32)[0:1]
    row = iota((TR, ENT), 0)
    spread = jnp.where(row == offset[...], w0, 0.0)
    spread += jnp.where(row == offset[...] + 1, jnp.where(count[...] > 1, w1 + 16.0, 0.0), 0.0)
    o32[pl.ds(15, DEV, stride=16), :] = lax.dot_general(
        onehot, spread.astype(BF), (((1,), (1,)), ((), ())), preferred_element_type=F32
    )
    out[...] = o32[...].astype(BF).reshape(DEV, 16, 128)


def build_stem(stem_w, wf, wide):
    wf[...] = jnp.zeros(wf.shape, F32)
    taps = stem_w[...].astype(F32)
    for a in range(3):
        for j in range(8):
            wf[128 * a + 12 * j : 128 * a + 12 * j + 18, 128 * j : 128 * j + 128] = taps[18 * a : 18 * a + 18]
    wide[...] = wf[...].astype(BF)


def blend(arrived, r32, wide, bias, b32, strips):
    r32[...] = arrived[...].astype(F32).reshape(DEV * 16, 128)

    def chunk(r):
        return r32[pl.ds(r, DEV, stride=16), :]

    lane = iota((DEV, 128), 1)
    windows = []
    for p in range(5):
        c0, c1, c2 = chunk(3 * p), chunk(3 * p + 1), chunk(3 * p + 2)
        w0 = jnp.where(lane < 6, 0.0, pltpu.roll(c0, 6, 1))
        w1 = jnp.where(lane < 38, pltpu.roll(c0, 38, 1), pltpu.roll(c1, 38, 1))
        w2 = jnp.where(lane < 70, pltpu.roll(c1, 70, 1), pltpu.roll(c2, 70, 1))
        w3 = pltpu.roll(c2, 102, 1)
        windows.append([w.astype(BF) for w in (w0, w1, w2, w3)])
    code = chunk(15)
    first = jnp.where(code <= 8.0, code, 0.0)
    second = jnp.where(code > 8.0, code - 16.0, 0.0)
    weights = jnp.concatenate([first, second], axis=0).astype(BF)
    contract = (((0,), (0,)), ((), ()))
    total = lax.dot_general(weights, jnp.ones((256, 128), BF), contract, preferred_element_type=F32)
    inverse = 1.0 / jnp.maximum(total, 1.0)
    wide_bias = jnp.concatenate([bias[...]] * 8, axis=1)
    for m in range(4):
        pixels = jnp.concatenate(
            [jnp.concatenate([windows[2 * i + a][m] for a in range(3)], axis=1) for i in range(2)], axis=0
        )
        summed = jnp.dot(pixels, wide[...], preferred_element_type=F32) + wide_bias
        features = jnp.maximum(summed, 0.0).astype(BF)
        numerator = lax.dot_general(weights, features, contract, preferred_element_type=F32)
        for j in range(8):
            column = 8 * m + j
            value = (numerator[:, 128 * j : 128 * j + 128] * inverse).astype(BF)
            start = (column + 2) * PITCH1 + 8
            b32[start : start + TR] = value.astype(F32)
            if column < 2:
                strips[column] = value
            if column >= TW - 2:
                strips[column - TW + 4] = value


def kernel(
    scene_h, tile_h, offset_h, count_h, rweight_h, stem_w_h, bias_h,
    w1_h, scale1_h, shift1_h, w2_h, scale2_h, shift2_h, out_h,
    scene, tile, offset, count, rweight, stem_w, bias, w1, scale1, shift1, w2, scale2, shift2,
    s32, o32, send, recv, r32, wf, wide, b32, strips, edges, got_strips, got_edges, got_corners,
    l1, h32, l2, out,
    in_sem, small_sem, w_sem, a2a_send, a2a_recv, halo_send, halo_recv, ready, out_sem,
):
    tx, ty = lax.axis_index("tx"), lax.axis_index("ty")
    me = tx * NY + ty

    small = [
        (tile_h, tile), (offset_h, offset), (count_h, count), (rweight_h, rweight), (stem_w_h, stem_w), (bias_h, bias),
        (scale1_h, scale1), (shift1_h, shift1), (scale2_h, scale2), (shift2_h, shift2),
    ]
    loads = [pltpu.make_async_copy(scene_h, scene, in_sem)]
    loads += [pltpu.make_async_copy(a, b, small_sem.at[n]) for n, (a, b) in enumerate(small)]
    for copy in loads:
        copy.start()
    weight_loads = []
    for a in range(3):
        for b in range(3):
            source, target = (3 * a + b) * C1, (3 * b + a) * C1
            weight_loads.append(
                pltpu.make_async_copy(w1_h.at[pl.ds(source, C1)], w1.at[pl.ds(target, C1)], w_sem.at[3 * a + b])
            )
    weight_loads.append(pltpu.make_async_copy(w2_h, w2, w_sem.at[9]))
    for copy in weight_loads:
        copy.start()

    barrier = pltpu.get_barrier_semaphore()

    def greet(semaphore, other_tx, other_ty):
        pl.semaphore_signal(semaphore, inc=1, device_id=(other_tx, other_ty), device_id_type=MESH)

    for n in range(1, NX):
        greet(barrier, lax.rem(tx + n, NX), ty)
    for n in range(1, NY):
        greet(barrier, tx, lax.rem(ty + n, NY))

    for copy in loads:
        copy.wait()
    pack_messages(scene, tile, offset, count, rweight, s32, o32, send)

    pl.semaphore_wait(barrier, NX + NY - 2)
    for n in range(1, NX):
        greet(ready, lax.rem(tx + n, NX), ty)
    pl.semaphore_wait(ready, NX - 1)

    def send_one(n, carry):
        other = lax.rem(me + n, DEV)
        pltpu.make_async_remote_copy(
            send.at[other], recv.at[me], a2a_send, a2a_recv,
            device_id=(lax.div(other, NY), lax.rem(other, NY)), device_id_type=MESH,
        ).start()
        return carry

    lax.fori_loop(1, DEV, send_one, 0)
    recv[me] = send[me]
    build_stem(stem_w, wf, wide)
    others = pl.ds(0, DEV - 1)
    pltpu.make_async_remote_copy(
        send.at[others], recv.at[others], a2a_send, a2a_recv, device_id=(tx, ty), device_id_type=MESH
    ).wait()

    blend(recv, r32, wide, bias, b32, strips)

    for side in range(2):
        for r in range(2):
            row = 8 + r + side * (TR - 2)
            edges[side, r] = b32[pl.ds(2 * PITCH1 + row, TW, stride=PITCH1), :].astype(BF)
    up, down = lax.rem(tx + NX - 1, NX), lax.rem(tx + 1, NX)
    left, right = lax.rem(ty + NY - 1, NY), lax.rem(ty + 1, NY)
    half = TW // 2
    near, far = pl.ds(0, half), pl.ds(half, half)
    moves = [
        (edges.at[1], got_edges.at[0], (down, ty)),
        (edges.at[0], got_edges.at[1], (up, ty)),
        (strips.at[pl.ds(2, 2)], got_strips.at[0], (tx, right)),
        (strips.at[pl.ds(0, 2)], got_strips.at[1], (tx, left)),
        (edges.at[1, :, far], got_corners.at[0], (down, right)),
        (edges.at[1, :, near], got_corners.at[1], (down, left)),
        (edges.at[0, :, far], got_corners.at[2], (up, right)),
        (edges.at[0, :, near], got_corners.at[3], (up, left)),
    ]
    halo = [
        pltpu.make_async_remote_copy(
            source, target, halo_send.at[n], halo_recv.at[n], device_id=device, device_id_type=MESH
        )
        for n, (source, target, device) in enumerate(moves)
    ]
    for copy in halo:
        copy.start()
    for copy in halo:
        copy.wait()

    has_up, has_down = tx > 0, tx < NX - 1
    has_left, has_right = ty > 0, ty < NY - 1
    for side, inside in ((0, has_up), (1, has_down)):
        for r in range(2):
            row = 6 + r + side * (TR + 2)
            line = jnp.where(inside, got_edges[side, r].astype(F32), 0.0)
            b32[pl.ds(2 * PITCH1 + row, TW, stride=PITCH1), :] = line
    for side, inside in ((0, has_left), (1, has_right)):
        for c in range(2):
            start = (c + side * (TW + 2)) * PITCH1
            strip = jnp.where(inside, got_strips[side, c].astype(F32), 0.0)
            b32[start + 8 : start + 8 + TR] = strip
    for corner in range(4):
        lower, to_left = corner >= 2, corner % 2 == 0
        inside = (has_down if lower else has_up) & (has_left if to_left else has_right)
        for r in range(2):
            values = jnp.where(inside, got_corners[corner, r].astype(F32), 0.0)
            for c in range(2):
                column = c if to_left else TW + 2 + c
                picked = half - 2 + c if to_left else c
                at = column * PITCH1 + 6 + r + (TR + 2 if lower else 0)
                b32[at : at + 1] = values[picked : picked + 1]

    def lay_column(t, carry):
        start = pl.multiple_of(t * PITCH1, 8)
        for a in range(3):
            l1[t, :, 128 * a : 128 * a + 128] = b32[pl.ds(start + 6 + a, 144), :].astype(BF)
        return carry

    lax.fori_loop(0, TW + 4, lay_column, 0)

    for copy in weight_loads:
        copy.wait()

    rows = iota((144, C2), 0)
    keep_rows = ((rows > 0) | has_up) & ((rows < TR + 1) | has_down)

    def first_conv(t, carry):
        pixels = jnp.concatenate([l1[t], l1[t + 1], l1[t + 2]], axis=1)
        summed = jnp.dot(pixels, w1[...], preferred_element_type=F32)
        value = jnp.maximum(summed * scale1[...] + shift1[...], 0.0).astype(BF).astype(F32)
        inside = ((t > 0) | has_left) & ((t < TW + 1) | has_right)
        value = jnp.where(keep_rows & inside, value, 0.0)
        for c in range(2):
            h32[c, pl.ds(t, TR + 2, stride=PITCH2), :] = value[: TR + 2, 128 * c : 128 * c + 128]
        return carry

    lax.fori_loop(0, TW + 2, first_conv, 0)

    def lay_row(h, carry):
        start = pl.multiple_of(h * PITCH2, 8)
        for b in range(3):
            for c in range(2):
                lanes = 256 * b + 128 * c
                l2[h, :, lanes : lanes + 128] = h32[c, pl.ds(start + b, TW), :].astype(BF)
        return carry

    lax.fori_loop(0, TR + 2, lay_row, 0)

    def second_conv(n, carry):
        y = n * MB
        summed = None
        for a in range(3):
            pixels = l2[pl.ds(y + a, MB)].reshape(MB * TW, 3 * C2)
            part = jnp.dot(pixels, w2[3 * C2 * a : 3 * C2 * (a + 1)], preferred_element_type=F32)
            summed = part if a == 0 else summed + part
        value = jnp.maximum(summed * scale2[...] + shift2[...], 0.0).astype(BF)
        out[pl.ds(y, MB)] = value.reshape(MB, TW, C2)
        pltpu.make_async_copy(out.at[pl.ds(y, MB)], out_h.at[pl.ds(y, MB)], out_sem.at[n]).start()
        return carry

    lax.fori_loop(0, TR // MB, second_conv, 0)
    for n in range(TR // MB):
        pltpu.make_async_copy(out.at[pl.ds(n * MB, MB)], out_h.at[pl.ds(n * MB, MB)], out_sem.at[n]).wait()


def per_device(
    scenes, foot_tile, foot_offset, foot_count, row_weight, stem_weight, stem_bias,
    first_weight, first_scale, first_shift, second_weight, second_scale, second_shift,
):
    args = (
        scenes.reshape(2 * TR, 3 * 128),
        foot_tile.reshape(1, ENT),
        foot_offset.reshape(1, ENT),
        foot_count.reshape(1, ENT),
        row_weight.reshape(1, 128),
        stem_weight,
        stem_bias.reshape(1, C1),
        first_weight,
        first_scale.reshape(1, C2),
        first_shift.reshape(1, C2),
        second_weight,
        second_scale.reshape(1, C2),
        second_shift.reshape(1, C2),
    )
    dma = pltpu.SemaphoreType.DMA
    v = pltpu.VMEM
    scratch = [v(x.shape, x.dtype) for x in args]
    scratch += [
        v((3, 264, 128), F32), v((DEV * 16, 128), F32), v((DEV, 16, 128), BF), v((DEV, 16, 128), BF),
        v((DEV * 16, 128), F32), v((384, 1024), F32), v((384, 1024), BF),
        v(((TW + 4) * PITCH1, 128), F32), v((4, TR, 128), BF), v((2, 2, TW, 128), BF),
        v((2, 2, TR, 128), BF), v((2, 2, TW, 128), BF), v((4, 2, TW // 2, 128), BF),
        v((TW + 4, 144, 384), BF), v((2, (TR + 2) * PITCH2, 128), F32), v((TR + 2, TW, 3 * C2), BF),
        v((TR, TW, C2), BF),
        dma, dma((10,)), dma((10,)), dma, dma, dma((8,)), dma((8,)), pltpu.SemaphoreType.REGULAR, dma((TR // MB,)),
    ]
    return pl.pallas_call(
        kernel,
        out_shape=jax.ShapeDtypeStruct((TR, TW, C2), BF),
        in_specs=[pl.BlockSpec(memory_space=pl.ANY)] * len(args),
        out_specs=pl.BlockSpec(memory_space=pl.ANY),
        scratch_shapes=scratch,
        compiler_params=pltpu.CompilerParams(
            collective_id=0, has_side_effects=True, vmem_limit_bytes=56 * 1024 * 1024
        ),
        cost_estimate=pl.CostEstimate(flops=7_500_000_000, bytes_accessed=6_000_000, transcendentals=0),
    )(*args)


def solution(mesh):
    shared = P()
    split = P(("tx", "ty"))
    in_specs = (P(("tx", "ty"), None, None), split, split, split, split) + (shared,) * 8
    return jax.shard_map(
        per_device, mesh=mesh, in_specs=in_specs, out_specs=P("tx", "ty", None), check_vma=False
    )
```

time: 280 us -> 50 us (0.18); the launches traced: 276 us -> 49.5 us
  waiting for transfers between devices: 99.4 us -> 0 us
  blocking collectives: 61.8 us -> 0 us
  Pallas kernels: 0 us -> 46.4 us
  local copies, waits for them, and re-layouts: 37.9 us -> 3.08 us
  starting transfers between devices: 29.7 us -> 0 us
  matrix products: 19.3 us -> 0 us
  between operations: 14.1 us -> 0.01 us
  other arithmetic: 13.7 us -> 0 us
    unnamed x2 -> x0, waiting for transfers between devices: 88.7 us -> none
    all_gather x1 -> x0, blocking collectives: 61.8 us -> none  [per_device(): lax.all_gather(row_weight, ('tx', 'ty'), axis=0, tiled=True)]
    pallas_call x0 -> x1, Pallas kernels: none -> 46.4 us  [per_device(): pl.pallas_call(kernel, out_shape=jax.ShapeDtypeStruct((TR, TW, C2), BF),...]
    dot_general x20 -> x0, matrix products: 19.3 us -> none  [the longest x18 16.8 us: conv_layer(): jnp.dot(window, kernel[shift_row, shift_col], preferred_element_type=jnp....]
    ppermute x8 -> x0, starting transfers between devices: 18.2 us -> none  [the longest x4 11.6 us: padded_2(): before = lax.ppermute(last, axis, up)]
    concatenate x5 -> x0, local copies, waits for them, and re-layouts: 16.6 us -> none  [the longest x4 16.6 us: make_strips(): strips = jnp.concatenate([row_pairs, third_rows[:, :, None, :]], axis=2)]
    all_to_all x1 -> x0, starting transfers between devices: 11.5 us -> none  [per_device(): lax.all_to_all(outgoing, ('tx', 'ty'), split_axis=0, concat_axis=0, tiled...]
    ppermute x8 -> x0, waiting for transfers between devices: 10.7 us -> none  [the longest x4 10.7 us: padded_2(): after = lax.ppermute(leading, axis, down)]
  transfers between devices with their start and end apart: 10 -> 0, of which waited for: 5 -> 0; matrix products, arithmetic and copies ran while one was open for 3% -> 0% of each run, Pallas kernels for 0% -> 0%
where the time goes in v1:
time: 50 us; the launch traced here: 49.5 us
  Pallas kernels  46.4 us (93%)
  local copies, waits for them, and re-layouts  3.08 us (6%)
    pallas_call x1, Pallas kernels, per_device(): pl.pallas_call(kernel, out_shape=jax.ShapeDtypeStruct((TR, TW, C2), BF),...  46.4 us
    unnamed x1, local copies, waits for them, and re-layouts  3.08 us

profile of v1, /device:TPU:1, one launch (start us, length us, event | category | flops | bytes accessed | tf_op | source)
XLA Modules:
  0.0 49.5 jit_solution(16026432033199661384)
XLA Ops:
  0.0 46.4 %shard_map.127 = bf16[128,32,256]{2,1,0:T(8,128)(2,1)} custom-call(bf16[256,384]{1,0:T(8,128)(2,1)} %bitcast.10, s32[1,64]{1,0:T(1,128)} %bitcast.15, s32[1,64]{1,0:T(1,128)} %bitcast.16, s32[1,64]{1,0:T(1,128)} %bitcast.17, s32[1,128]{1,0:T(1,128)} %bitcast.18, bf16[54,128]{1,0:T(8,128)(2,1)} %stem_w_h.1, f32[1,128]{1,0:T(1,128)} %bitcast.19, ...), custom_call_target="tpu_custom_call" | custom-call | flops 7500000256 | bytes 6000000 | tf_op jit(solution)/shard_map/pallas_call | solution.py:307
  46.4 3.1 %copy.15 = bf16[128,32,256]{2,1,0:T(8,128)(2,1)} copy(bf16[128,32,256]{2,1,0:T(8,128)(2,1)} %shard_map.127) | data formatting | bytes 4194304

commit v2 on v1

--- a/solution.py
+++ b/solution.py
@@ -12,13 +12,24 @@
 C1, C2 = 128, 256
 PITCH1 = 152
 PITCH2 = 40
-MB = 32
+CB = 17
+MB = 64
 BF, F32 = jnp.bfloat16, jnp.float32
 MESH = pl.DeviceIdType.MESH
 
 
 def iota(shape, dim):
     return lax.broadcasted_iota(jnp.int32, shape, dim)
+
+
+def far_first(tx, ty):
+    y, core = tx // 2, lax.rem(tx, 2)
+    z, x = ty // 4, lax.rem(ty, 4)
+    ys, zs, xs = ([lax.rem(at + d, 4) for d in range(4)] for at in (y, z, x))
+    cores = [core, 1 - core]
+    steps = [(a, b, c, d) for a in range(4) for b in range(4) for c in range(4) for d in range(2)][1:]
+    steps.sort(key=lambda s: (-sum(min(n, 4 - n) for n in s[:3]), s[3], s))
+    return [(ys[a] * 2 + cores[d], zs[b] * 4 + xs[c]) for a, b, c, d in steps]
 
 
 def pack_messages(scene, tile, offset, count, rweight, s32, o32, out):
@@ -103,18 +114,18 @@
 
 def kernel(
     scene_h, tile_h, offset_h, count_h, rweight_h, stem_w_h, bias_h,
-    w1_h, scale1_h, shift1_h, w2_h, scale2_h, shift2_h, out_h,
-    scene, tile, offset, count, rweight, stem_w, bias, w1, scale1, shift1, w2, scale2, shift2,
+    w1_h, scale1_h, shift1_h, l2,
+    scene, tile, offset, count, rweight, stem_w, bias, w1, scale1, shift1,
     s32, o32, send, recv, r32, wf, wide, b32, strips, edges, got_strips, got_edges, got_corners,
-    l1, h32, l2, out,
-    in_sem, small_sem, w_sem, a2a_send, a2a_recv, halo_send, halo_recv, ready, out_sem,
+    l1, h32,
+    in_sem, small_sem, w_sem, a2a_send, a2a_recv, halo_send, halo_recv,
 ):
     tx, ty = lax.axis_index("tx"), lax.axis_index("ty")
     me = tx * NY + ty
 
     small = [
         (tile_h, tile), (offset_h, offset), (count_h, count), (rweight_h, rweight), (stem_w_h, stem_w), (bias_h, bias),
-        (scale1_h, scale1), (shift1_h, shift1), (scale2_h, scale2), (shift2_h, shift2),
+        (scale1_h, scale1), (shift1_h, shift1),
     ]
     loads = [pltpu.make_async_copy(scene_h, scene, in_sem)]
     loads += [pltpu.make_async_copy(a, b, small_sem.at[n]) for n, (a, b) in enumerate(small)]
@@ -127,44 +138,30 @@
             weight_loads.append(
                 pltpu.make_async_copy(w1_h.at[pl.ds(source, C1)], w1.at[pl.ds(target, C1)], w_sem.at[3 * a + b])
             )
-    weight_loads.append(pltpu.make_async_copy(w2_h, w2, w_sem.at[9]))
     for copy in weight_loads:
         copy.start()
 
     barrier = pltpu.get_barrier_semaphore()
-
-    def greet(semaphore, other_tx, other_ty):
-        pl.semaphore_signal(semaphore, inc=1, device_id=(other_tx, other_ty), device_id_type=MESH)
-
-    for n in range(1, NX):
-        greet(barrier, lax.rem(tx + n, NX), ty)
-    for n in range(1, NY):
-        greet(barrier, tx, lax.rem(ty + n, NY))
+    places = far_first(tx, ty)
+    for place in places:
+        pl.semaphore_signal(barrier, inc=1, device_id=place, device_id_type=MESH)
 
     for copy in loads:
         copy.wait()
     pack_messages(scene, tile, offset, count, rweight, s32, o32, send)
 
-    pl.semaphore_wait(barrier, NX + NY - 2)
-    for n in range(1, NX):
-        greet(ready, lax.rem(tx + n, NX), ty)
-    pl.semaphore_wait(ready, NX - 1)
-
-    def send_one(n, carry):
-        other = lax.rem(me + n, DEV)
+    pl.semaphore_wait(barrier, DEV - 1)
+    for place in places:
         pltpu.make_async_remote_copy(
-            send.at[other], recv.at[me], a2a_send, a2a_recv,
-            device_id=(lax.div(other, NY), lax.rem(other, NY)), device_id_type=MESH,
+            send.at[place[0] * NY + place[1]], recv.at[me], a2a_send, a2a_recv, device_id=place, device_id_type=MESH
         ).start()
-        return carry
-
-    lax.fori_loop(1, DEV, send_one, 0)
     recv[me] = send[me]
     build_stem(stem_w, wf, wide)
     others = pl.ds(0, DEV - 1)
-    pltpu.make_async_remote_copy(
+    exchange = pltpu.make_async_remote_copy(
         send.at[others], recv.at[others], a2a_send, a2a_recv, device_id=(tx, ty), device_id_type=MESH
-    ).wait()
+    )
+    exchange.wait_recv()
 
     blend(recv, r32, wide, bias, b32, strips)
 
@@ -172,33 +169,31 @@
         for r in range(2):
             row = 8 + r + side * (TR - 2)
             edges[side, r] = b32[pl.ds(2 * PITCH1 + row, TW, stride=PITCH1), :].astype(BF)
-    up, down = lax.rem(tx + NX - 1, NX), lax.rem(tx + 1, NX)
-    left, right = lax.rem(ty + NY - 1, NY), lax.rem(ty + 1, NY)
+    has_up, has_down = tx > 0, tx < NX - 1
+    has_left, has_right = ty > 0, ty < NY - 1
     half = TW // 2
     near, far = pl.ds(0, half), pl.ds(half, half)
     moves = [
-        (edges.at[1], got_edges.at[0], (down, ty)),
-        (edges.at[0], got_edges.at[1], (up, ty)),
-        (strips.at[pl.ds(2, 2)], got_strips.at[0], (tx, right)),
-        (strips.at[pl.ds(0, 2)], got_strips.at[1], (tx, left)),
-        (edges.at[1, :, far], got_corners.at[0], (down, right)),
-        (edges.at[1, :, near], got_corners.at[1], (down, left)),
-        (edges.at[0, :, far], got_corners.at[2], (up, right)),
-        (edges.at[0, :, near], got_corners.at[3], (up, left)),
+        (strips.at[pl.ds(2, 2)], got_strips.at[0], (0, 1), has_right, has_left),
+        (strips.at[pl.ds(0, 2)], got_strips.at[1], (0, -1), has_left, has_right),
+        (edges.at[1, :, far], got_corners.at[0], (1, 1), has_down & has_right, has_up & has_left),
+        (edges.at[1, :, near], got_corners.at[1], (1, -1), has_down & has_left, has_up & has_right),
+        (edges.at[0, :, far], got_corners.at[2], (-1, 1), has_up & has_right, has_down & has_left),
+        (edges.at[0, :, near], got_corners.at[3], (-1, -1), has_up & has_left, has_down & has_right),
+        (edges.at[1], got_edges.at[0], (1, 0), has_down, has_up),
+        (edges.at[0], got_edges.at[1], (-1, 0), has_up, has_down),
     ]
-    halo = [
-        pltpu.make_async_remote_copy(
-            source, target, halo_send.at[n], halo_recv.at[n], device_id=device, device_id_type=MESH
+    halo = []
+    for n, (source, target, (down, right), sends, receives) in enumerate(moves):
+        place = (lax.rem(tx + down + NX, NX), lax.rem(ty + right + NY, NY))
+        copy = pltpu.make_async_remote_copy(
+            source, target, halo_send.at[n], halo_recv.at[n], device_id=place, device_id_type=MESH
         )
-        for n, (source, target, device) in enumerate(moves)
-    ]
-    for copy in halo:
-        copy.start()
-    for copy in halo:
-        copy.wait()
-
-    has_up, has_down = tx > 0, tx < NX - 1
-    has_left, has_right = ty > 0, ty < NY - 1
+        pl.when(sends)(copy.start)
+        halo.append((copy, sends, receives))
+    for copy, _, receives in halo:
+        pl.when(receives)(copy.wait_recv)
+
     for side, inside in ((0, has_up), (1, has_down)):
         for r in range(2):
             row = 6 + r + side * (TR + 2)
@@ -234,17 +229,19 @@
     rows = iota((144, C2), 0)
     keep_rows = ((rows > 0) | has_up) & ((rows < TR + 1) | has_down)
 
-    def first_conv(t, carry):
-        pixels = jnp.concatenate([l1[t], l1[t + 1], l1[t + 2]], axis=1)
+    def first_conv(step, carry):
+        t = step * CB
+        pixels = jnp.concatenate([l1[pl.ds(t + b, CB)].reshape(CB * 144, 3 * C1) for b in range(3)], axis=1)
         summed = jnp.dot(pixels, w1[...], preferred_element_type=F32)
         value = jnp.maximum(summed * scale1[...] + shift1[...], 0.0).astype(BF).astype(F32)
-        inside = ((t > 0) | has_left) & ((t < TW + 1) | has_right)
-        value = jnp.where(keep_rows & inside, value, 0.0)
-        for c in range(2):
-            h32[c, pl.ds(t, TR + 2, stride=PITCH2), :] = value[: TR + 2, 128 * c : 128 * c + 128]
+        for n in range(CB):
+            inside = ((t + n > 0) | has_left) & ((t + n < TW + 1) | has_right)
+            kept = jnp.where(keep_rows & inside, value[144 * n : 144 * n + 144], 0.0)
+            for c in range(2):
+                h32[c, pl.ds(t + n, TR + 2, stride=PITCH2), :] = kept[: TR + 2, 128 * c : 128 * c + 128]
         return carry
 
-    lax.fori_loop(0, TW + 2, first_conv, 0)
+    lax.fori_loop(0, (TW + 2) // CB, first_conv, 0)
 
     def lay_row(h, carry):
         start = pl.multiple_of(h * PITCH2, 8)
@@ -256,7 +253,17 @@
 
     lax.fori_loop(0, TR + 2, lay_row, 0)
 
-    def second_conv(n, carry):
+    exchange.wait_send()
+    for copy, sends, _ in halo:
+        pl.when(sends)(copy.wait_send)
+
+
+def second_kernel(l2, w2, scale2, shift2, out_h, out, out_sem):
+    def move(n):
+        part = pl.ds(n * MB, MB)
+        return pltpu.make_async_copy(out.at[part], out_h.at[part], out_sem.at[n])
+
+    for n in range(TR // MB):
         y = n * MB
         summed = None
         for a in range(3):
@@ -265,12 +272,9 @@
             summed = part if a == 0 else summed + part
         value = jnp.maximum(summed * scale2[...] + shift2[...], 0.0).astype(BF)
         out[pl.ds(y, MB)] = value.reshape(MB, TW, C2)
-        pltpu.make_async_copy(out.at[pl.ds(y, MB)], out_h.at[pl.ds(y, MB)], out_sem.at[n]).start()
-        return carry
-
-    lax.fori_loop(0, TR // MB, second_conv, 0)
+        move(n).start()
     for n in range(TR // MB):
-        pltpu.make_async_copy(out.at[pl.ds(n * MB, MB)], out_h.at[pl.ds(n * MB, MB)], out_sem.at[n]).wait()
+        move(n).wait()
 
 
 def per_device(
@@ -288,9 +292,6 @@
         first_weight,
         first_scale.reshape(1, C2),
         first_shift.reshape(1, C2),
-        second_weight,
-        second_scale.reshape(1, C2),
-        second_shift.reshape(1, C2),
     )
     dma = pltpu.SemaphoreType.DMA
     v = pltpu.VMEM
@@ -300,21 +301,29 @@
         v((DEV * 16, 128), F32), v((384, 1024), F32), v((384, 1024), BF),
         v(((TW + 4) * PITCH1, 128), F32), v((4, TR, 128), BF), v((2, 2, TW, 128), BF),
         v((2, 2, TR, 128), BF), v((2, 2, TW, 128), BF), v((4, 2, TW // 2, 128), BF),
-        v((TW + 4, 144, 384), BF), v((2, (TR + 2) * PITCH2, 128), F32), v((TR + 2, TW, 3 * C2), BF),
-        v((TR, TW, C2), BF),
-        dma, dma((10,)), dma((10,)), dma, dma, dma((8,)), dma((8,)), pltpu.SemaphoreType.REGULAR, dma((TR // MB,)),
+        v((TW + 4, 144, 384), BF), v((2, (TR + 2) * PITCH2, 128), F32),
+        dma, dma((8,)), dma((9,)), dma, dma, dma((8,)), dma((8,)),
     ]
-    return pl.pallas_call(
+    hidden = pl.pallas_call(
         kernel,
-        out_shape=jax.ShapeDtypeStruct((TR, TW, C2), BF),
-        in_specs=[pl.BlockSpec(memory_space=pl.ANY)] * len(args),
-        out_specs=pl.BlockSpec(memory_space=pl.ANY),
+        out_shape=jax.ShapeDtypeStruct((TR + 2, TW, 3 * C2), BF),
+        in_specs=[pl.BlockSpec(memory_space=pltpu.HBM)] * len(args),
+        out_specs=pl.BlockSpec(memory_space=v),
         scratch_shapes=scratch,
         compiler_params=pltpu.CompilerParams(
-            collective_id=0, has_side_effects=True, vmem_limit_bytes=56 * 1024 * 1024
+            collective_id=0, has_side_effects=True, vmem_limit_bytes=44 * 1024 * 1024
         ),
-        cost_estimate=pl.CostEstimate(flops=7_500_000_000, bytes_accessed=6_000_000, transcendentals=0),
-    )(*args)
+        cost_estimate=pl.CostEstimate(flops=2_700_000_000, bytes_accessed=2_000_000, transcendentals=0),
+    )(*[pltpu.with_memory_space_constraint(x, pltpu.HBM) for x in args])
+    return pl.pallas_call(
+        second_kernel,
+        out_shape=jax.ShapeDtypeStruct((TR, TW, C2), BF),
+        in_specs=[pl.BlockSpec(memory_space=v)] * 4,
+        out_specs=pl.BlockSpec(memory_space=pl.ANY),
+        scratch_shapes=[v((TR, TW, C2), BF), dma((TR // MB,))],
+        compiler_params=pltpu.CompilerParams(vmem_limit_bytes=32 * 1024 * 1024),
+        cost_estimate=pl.CostEstimate(flops=4_800_000_000, bytes_accessed=3_000_000, transcendentals=0),
+    )(hidden, second_weight, second_scale.reshape(1, C2), second_shift.reshape(1, C2))
 
 
 def solution(mesh):

time: 50 us -> 37.6 us (0.75)
  Pallas kernels: 46.4 us -> 37.4 us
  local copies, waits for them, and re-layouts: 3.08 us -> 0.01 us
    pallas_call x1 -> x2, Pallas kernels: 46.4 us -> 37.4 us  [the longest x1 30.9 us: per_device(): pl.pallas_call(kernel, out_shape=jax.ShapeDtypeStruct((TR + 2, TW, 3 * C2...]
    unnamed x1 -> x6, local copies, waits for them, and re-layouts: 3.08 us -> 0.01 us
where the time goes in v2:
time: 37.6 us; the launch traced here: 37.5 us
  Pallas kernels  37.4 us (99%)
    pallas_call x1, Pallas kernels, per_device(): pl.pallas_call(kernel, out_shape=jax.ShapeDtypeStruct((TR + 2, TW, 3 * C2...  30.9 us
    pallas_call x1, Pallas kernels, per_device(): pl.pallas_call(second_kernel, out_shape=jax.ShapeDtypeStruct((TR, TW, C2)...  6.5 us

profile of v2, /device:TPU:1, one launch (start us, length us, event | category | flops | bytes accessed | tf_op | source)
XLA Modules:
  0.0 37.5 jit_solution(8304523111900179253)
XLA Ops:
  0.0 0.0 copy-start
  0.0 0.0 copy-start.1
  0.0 0.0 copy-start.2
  0.0 30.9 %shard_map.127.l2 = bf16[130,32,768]{2,1,0:T(8,128)(2,1)S(1)} custom-call(bf16[256,384]{1,0:T(8,128)(2,1)} %bitcast.12, s32[1,64]{1,0:T(1,128)} %bitcast.15, s32[1,64]{1,0:T(1,128)} %bitcast.16, s32[1,64]{1,0:T(1,128)} %bitcast.17, s32[1,128]{1,0:T(1,128)} %bitcast.18, bf16[54,128]{1,0:T(8,128)(2,1)} %stem_w_h.1, f32[1,128]{1,0:T(1,128)} %bitcast.19, ...), custom_call_target="tpu_custom_call" | custom-call | flops 2700000000 | bytes 2000000 | tf_op jit(solution)/shard_map/pallas_call | solution.py:307
  31.0 0.0 copy-done
  31.0 0.0 copy-done.1
  31.0 0.0 copy-done.2
  31.0 6.5 %shard_map.128 = bf16[128,32,256]{2,1,0:T(8,128)(2,1)} custom-call(bf16[130,32,768]{2,1,0:T(8,128)(2,1)S(1)} %shard_map.127.l2, bf16[2304,256]{1,0:T(8,128)(2,1)S(1)} %copy-done, f32[1,256]{1,0:T(1,128)S(1)} %bitcast.10, f32[1,256]{1,0:T(1,128)S(1)} %bitcast.11), custom_call_target="tpu_custom_call" | custom-call | flops 4800000000 | bytes 3000000 | tf_op jit(solution)/shard_map/pallas_call | solution.py:318
Async XLA Ops:
  0.0 31.0 %copy-start = (bf16[2304,256]{1,0:T(8,128)(2,1)S(1)}, bf16[2304,256]{1,0:T(8,128)(2,1)}, u32[]{:S(2)}) copy-start(bf16[2304,256]{1,0:T(8,128)(2,1)} %w2.1) | copy-start | bytes 3538948
  0.0 31.0 %copy-start.1 = (f32[256]{0:T(256)S(1)}, f32[256]{0:T(256)}, u32[]{:S(2)}) copy-start(f32[256]{0:T(256)} %param.24) | copy-start | bytes 3076
  0.0 31.0 %copy-start.2 = (f32[256]{0:T(256)S(1)}, f32[256]{0:T(256)}, u32[]{:S(2)}) copy-start(f32[256]{0:T(256)} %param.25) | copy-start | bytes 3076

commit v3 on v2

--- a/solution.py
+++ b/solution.py
@@ -12,8 +12,9 @@
 C1, C2 = 128, 256
 PITCH1 = 152
 PITCH2 = 40
-CB = 17
-MB = 64
+MID = 112
+CB = 15
+MB = 32
 BF, F32 = jnp.bfloat16, jnp.float32
 MESH = pl.DeviceIdType.MESH
 
@@ -117,7 +118,7 @@
     w1_h, scale1_h, shift1_h, l2,
     scene, tile, offset, count, rweight, stem_w, bias, w1, scale1, shift1,
     s32, o32, send, recv, r32, wf, wide, b32, strips, edges, got_strips, got_edges, got_corners,
-    l1, h32,
+    middle, ends, h32,
     in_sem, small_sem, w_sem, a2a_send, a2a_recv, halo_send, halo_recv,
 ):
     tx, ty = lax.axis_index("tx"), lax.axis_index("ty")
@@ -191,6 +192,44 @@
         )
         pl.when(sends)(copy.start)
         halo.append((copy, sends, receives))
+    def lay_middle(t):
+        for a in range(3):
+            start = pl.multiple_of(t * PITCH1, 8) + 22 + a
+            middle[t, :, 128 * a : 128 * a + 128] = b32[pl.ds(start, MID), :].astype(BF)
+
+    def lay_ends(t):
+        for a in range(3):
+            for n in range(2):
+                start = pl.multiple_of(t * PITCH1, 8) + 6 + a + 128 * n
+                ends[t, 16 * n : 16 * n + 16, 128 * a : 128 * a + 128] = b32[pl.ds(start, 16), :].astype(BF)
+
+    def first_conv(source, t, columns):
+        height = source.shape[1]
+        pixels = [source[pl.ds(t + b, columns)].reshape(columns * height, 3 * C1) for b in range(3)]
+        summed = jnp.dot(jnp.concatenate(pixels, axis=1), w1[...], preferred_element_type=F32)
+        value = jnp.maximum(summed * scale1[...] + shift1[...], 0.0).astype(BF).astype(F32)
+        return value.reshape(columns, height, C2)
+
+    def loop(start, stop, step, unroll):
+        def body(n, carry):
+            step(n)
+            return carry
+
+        lax.fori_loop(start, stop, body, 0, unroll=unroll)
+
+    loop(2, TW + 2, lay_middle, 5)
+    for copy in weight_loads:
+        copy.wait()
+
+    def middle_block(n):
+        t = 2 + n * CB
+        value = first_conv(middle, t, CB)
+        for m in range(CB):
+            for c in range(2):
+                h32[c, pl.ds(16 * PITCH2 + t + m, MID, stride=PITCH2), :] = value[m, :, 128 * c : 128 * c + 128]
+
+    loop(0, (TW - 2) // CB, middle_block, 1)
+
     for copy, _, receives in halo:
         pl.when(receives)(copy.wait_recv)
 
@@ -215,43 +254,40 @@
                 at = column * PITCH1 + 6 + r + (TR + 2 if lower else 0)
                 b32[at : at + 1] = values[picked : picked + 1]
 
-    def lay_column(t, carry):
-        start = pl.multiple_of(t * PITCH1, 8)
-        for a in range(3):
-            l1[t, :, 128 * a : 128 * a + 128] = b32[pl.ds(start + 6 + a, 144), :].astype(BF)
-        return carry
-
-    lax.fori_loop(0, TW + 4, lay_column, 0)
-
-    for copy in weight_loads:
-        copy.wait()
-
-    rows = iota((144, C2), 0)
-    keep_rows = ((rows > 0) | has_up) & ((rows < TR + 1) | has_down)
-
-    def first_conv(step, carry):
-        t = step * CB
-        pixels = jnp.concatenate([l1[pl.ds(t + b, CB)].reshape(CB * 144, 3 * C1) for b in range(3)], axis=1)
-        summed = jnp.dot(pixels, w1[...], preferred_element_type=F32)
-        value = jnp.maximum(summed * scale1[...] + shift1[...], 0.0).astype(BF).astype(F32)
-        for n in range(CB):
-            inside = ((t + n > 0) | has_left) & ((t + n < TW + 1) | has_right)
-            kept = jnp.where(keep_rows & inside, value[144 * n : 144 * n + 144], 0.0)
+    loop(0, TW + 4, lay_ends, 4)
+    for t in (0, 1, TW + 2, TW + 3):
+        lay_middle(t)
+
+    for t, inside in ((0, has_left), (TW, has_right)):
+        value = first_conv(middle, t, 2)
+        for m in range(2):
+            kept = value[m]
+            if t + m in (0, TW + 1):
+                kept = jnp.where(inside, kept, 0.0)
             for c in range(2):
-                h32[c, pl.ds(t + n, TR + 2, stride=PITCH2), :] = kept[: TR + 2, 128 * c : 128 * c + 128]
-        return carry
-
-    lax.fori_loop(0, (TW + 2) // CB, first_conv, 0)
-
-    def lay_row(h, carry):
+                h32[c, pl.ds(16 * PITCH2 + t + m, MID, stride=PITCH2), :] = kept[:, 128 * c : 128 * c + 128]
+
+    rows = iota((32, C2), 0)
+    keep_rows = ((rows > 0) | has_up) & ((rows < 17) | has_down)
+    value = first_conv(ends, 0, TW + 2)
+    for t in range(TW + 2):
+        keep = keep_rows
+        if t in (0, TW + 1):
+            keep = keep & (has_right if t else has_left)
+        kept = jnp.where(keep, value[t], 0.0)
+        for c in range(2):
+            lanes = slice(128 * c, 128 * c + 128)
+            h32[c, pl.ds(t, 16, stride=PITCH2), :] = kept[:16, lanes]
+            h32[c, pl.ds(128 * PITCH2 + t, 2, stride=PITCH2), :] = kept[16:18, lanes]
+
+    def lay_row(h):
         start = pl.multiple_of(h * PITCH2, 8)
         for b in range(3):
             for c in range(2):
                 lanes = 256 * b + 128 * c
                 l2[h, :, lanes : lanes + 128] = h32[c, pl.ds(start + b, TW), :].astype(BF)
-        return carry
-
-    lax.fori_loop(0, TR + 2, lay_row, 0)
+
+    loop(0, TR + 2, lay_row, 5)
 
     exchange.wait_send()
     for copy, sends, _ in halo:
@@ -301,7 +337,7 @@
         v((DEV * 16, 128), F32), v((384, 1024), F32), v((384, 1024), BF),
         v(((TW + 4) * PITCH1, 128), F32), v((4, TR, 128), BF), v((2, 2, TW, 128), BF),
         v((2, 2, TR, 128), BF), v((2, 2, TW, 128), BF), v((4, 2, TW // 2, 128), BF),
-        v((TW + 4, 144, 384), BF), v((2, (TR + 2) * PITCH2, 128), F32),
+        v((TW + 4, MID, 384), BF), v((TW + 4, 32, 384), BF), v((2, (TR + 2) * PITCH2, 128), F32),
         dma, dma((8,)), dma((9,)), dma, dma, dma((8,)), dma((8,)),
     ]
     hidden = pl.pallas_call(

time: 37.6 us -> 33.4 us (0.89)
  Pallas kernels: 37.4 us -> 33.2 us
    pallas_call x1, Pallas kernels: 30.9 us -> 27.2 us  [per_device(): pl.pallas_call(kernel, out_shape=jax.ShapeDtypeStruct((TR + 2, TW, 3 * C2...]
    pallas_call x1, Pallas kernels: 6.5 us -> 6.06 us  [per_device(): pl.pallas_call(second_kernel, out_shape=jax.ShapeDtypeStruct((TR, TW, C2)...]
where the time goes in v3:
time: 33.4 us; the launch traced here: 33.3 us
  Pallas kernels  33.2 us (99%)
    pallas_call x1, Pallas kernels, per_device(): pl.pallas_call(kernel, out_shape=jax.ShapeDtypeStruct((TR + 2, TW, 3 * C2...  27.2 us
    pallas_call x1, Pallas kernels, per_device(): pl.pallas_call(second_kernel, out_shape=jax.ShapeDtypeStruct((TR, TW, C2)...  6.06 us

profile of v3, /device:TPU:1, one launch (start us, length us, event | category | flops | bytes accessed | tf_op | source)
XLA Modules:
  0.0 33.3 jit_solution(6604208002099332049)
XLA Ops:
  0.0 0.0 copy-start
  0.0 0.0 copy-start.1
  0.0 0.0 copy-start.2
  0.0 27.2 %shard_map.127.l2 = bf16[130,32,768]{2,1,0:T(8,128)(2,1)S(1)} custom-call(bf16[256,384]{1,0:T(8,128)(2,1)} %bitcast.12, s32[1,64]{1,0:T(1,128)} %bitcast.15, s32[1,64]{1,0:T(1,128)} %bitcast.16, s32[1,64]{1,0:T(1,128)} %bitcast.17, s32[1,128]{1,0:T(1,128)} %bitcast.18, bf16[54,128]{1,0:T(8,128)(2,1)} %stem_w_h.1, f32[1,128]{1,0:T(1,128)} %bitcast.19, ...), custom_call_target="tpu_custom_call" | custom-call | flops 2700000000 | bytes 2000000 | tf_op jit(solution)/shard_map/pallas_call | solution.py:343
  27.2 0.0 copy-done
  27.2 0.0 copy-done.1
  27.2 0.0 copy-done.2
  27.2 6.1 %shard_map.128 = bf16[128,32,256]{2,1,0:T(8,128)(2,1)} custom-call(bf16[130,32,768]{2,1,0:T(8,128)(2,1)S(1)} %shard_map.127.l2, bf16[2304,256]{1,0:T(8,128)(2,1)S(1)} %copy-done, f32[1,256]{1,0:T(1,128)S(1)} %bitcast.10, f32[1,256]{1,0:T(1,128)S(1)} %bitcast.11), custom_call_target="tpu_custom_call" | custom-call | flops 4800000000 | bytes 3000000 | tf_op jit(solution)/shard_map/pallas_call | solution.py:354
Async XLA Ops:
  0.0 27.2 %copy-start = (bf16[2304,256]{1,0:T(8,128)(2,1)S(1)}, bf16[2304,256]{1,0:T(8,128)(2,1)}, u32[]{:S(2)}) copy-start(bf16[2304,256]{1,0:T(8,128)(2,1)} %w2.1) | copy-start | bytes 3538948
  0.0 27.2 %copy-start.1 = (f32[256]{0:T(256)S(1)}, f32[256]{0:T(256)}, u32[]{:S(2)}) copy-start(f32[256]{0:T(256)} %param.24) | copy-start | bytes 3076
  0.0 27.2 %copy-start.2 = (f32[256]{0:T(256)S(1)}, f32[256]{0:T(256)}, u32[]{:S(2)}) copy-start(f32[256]{0:T(256)} %param.25) | copy-start | bytes 3076

commit v4 on v3

--- a/solution.py
+++ b/solution.py
@@ -14,7 +14,7 @@
 PITCH2 = 40
 MID = 112
 CB = 15
-MB = 32
+PARTS = (32, 32, 32, 32)
 BF, F32 = jnp.bfloat16, jnp.float32
 MESH = pl.DeviceIdType.MESH
 
@@ -115,10 +115,10 @@
 
 def kernel(
     scene_h, tile_h, offset_h, count_h, rweight_h, stem_w_h, bias_h,
-    w1_h, scale1_h, shift1_h, l2,
+    w1_h, scale1_h, shift1_h, h32,
     scene, tile, offset, count, rweight, stem_w, bias, w1, scale1, shift1,
     s32, o32, send, recv, r32, wf, wide, b32, strips, edges, got_strips, got_edges, got_corners,
-    middle, ends, h32,
+    middle, ends,
     in_sem, small_sem, w_sem, a2a_send, a2a_recv, halo_send, halo_recv,
 ):
     tx, ty = lax.axis_index("tx"), lax.axis_index("ty")
@@ -280,37 +280,40 @@
             h32[c, pl.ds(t, 16, stride=PITCH2), :] = kept[:16, lanes]
             h32[c, pl.ds(128 * PITCH2 + t, 2, stride=PITCH2), :] = kept[16:18, lanes]
 
+    exchange.wait_send()
+    for copy, sends, _ in halo:
+        pl.when(sends)(copy.wait_send)
+
+
+def second_kernel(h32, w2, scale2, shift2, out_h, l2, out, out_sem):
+    def move(n, y, size):
+        part = pl.ds(y, size)
+        return pltpu.make_async_copy(out.at[part], out_h.at[part], out_sem.at[n])
+
     def lay_row(h):
-        start = pl.multiple_of(h * PITCH2, 8)
         for b in range(3):
             for c in range(2):
                 lanes = 256 * b + 128 * c
-                l2[h, :, lanes : lanes + 128] = h32[c, pl.ds(start + b, TW), :].astype(BF)
-
-    loop(0, TR + 2, lay_row, 5)
-
-    exchange.wait_send()
-    for copy, sends, _ in halo:
-        pl.when(sends)(copy.wait_send)
-
-
-def second_kernel(l2, w2, scale2, shift2, out_h, out, out_sem):
-    def move(n):
-        part = pl.ds(n * MB, MB)
-        return pltpu.make_async_copy(out.at[part], out_h.at[part], out_sem.at[n])
-
-    for n in range(TR // MB):
-        y = n * MB
+                l2[h, :, lanes : lanes + 128] = h32[c, h * PITCH2 + b : h * PITCH2 + b + TW, :].astype(BF)
+
+    y, laid = 0, 0
+    moves = []
+    for n, size in enumerate(PARTS):
+        for h in range(laid, y + size + 2):
+            lay_row(h)
+        laid = y + size + 2
         summed = None
         for a in range(3):
-            pixels = l2[pl.ds(y + a, MB)].reshape(MB * TW, 3 * C2)
+            pixels = l2[y + a : y + a + size].reshape(size * TW, 3 * C2)
             part = jnp.dot(pixels, w2[3 * C2 * a : 3 * C2 * (a + 1)], preferred_element_type=F32)
             summed = part if a == 0 else summed + part
         value = jnp.maximum(summed * scale2[...] + shift2[...], 0.0).astype(BF)
-        out[pl.ds(y, MB)] = value.reshape(MB, TW, C2)
-        move(n).start()
-    for n in range(TR // MB):
-        move(n).wait()
+        out[y : y + size] = value.reshape(size, TW, C2)
+        moves.append(move(n, y, size))
+        moves[-1].start()
+        y += size
+    for copy in moves:
+        copy.wait()
 
 
 def per_device(
@@ -337,12 +340,12 @@
         v((DEV * 16, 128), F32), v((384, 1024), F32), v((384, 1024), BF),
         v(((TW + 4) * PITCH1, 128), F32), v((4, TR, 128), BF), v((2, 2, TW, 128), BF),
         v((2, 2, TR, 128), BF), v((2, 2, TW, 128), BF), v((4, 2, TW // 2, 128), BF),
-        v((TW + 4, MID, 384), BF), v((TW + 4, 32, 384), BF), v((2, (TR + 2) * PITCH2, 128), F32),
+        v((TW + 4, MID, 384), BF), v((TW + 4, 32, 384), BF),
         dma, dma((8,)), dma((9,)), dma, dma, dma((8,)), dma((8,)),
     ]
     hidden = pl.pallas_call(
         kernel,
-        out_shape=jax.ShapeDtypeStruct((TR + 2, TW, 3 * C2), BF),
+        out_shape=jax.ShapeDtypeStruct((2, (TR + 2) * PITCH2, 128), F32),
         in_specs=[pl.BlockSpec(memory_space=pltpu.HBM)] * len(args),
         out_specs=pl.BlockSpec(memory_space=v),
         scratch_shapes=scratch,
@@ -356,7 +359,7 @@
         out_shape=jax.ShapeDtypeStruct((TR, TW, C2), BF),
         in_specs=[pl.BlockSpec(memory_space=v)] * 4,
         out_specs=pl.BlockSpec(memory_space=pl.ANY),
-        scratch_shapes=[v((TR, TW, C2), BF), dma((TR // MB,))],
+        scratch_shapes=[v((TR + 2, TW, 3 * C2), BF), v((TR, TW, C2), BF), dma((len(PARTS),))],
         compiler_params=pltpu.CompilerParams(vmem_limit_bytes=32 * 1024 * 1024),
         cost_estimate=pl.CostEstimate(flops=4_800_000_000, bytes_accessed=3_000_000, transcendentals=0),
     )(hidden, second_weight, second_scale.reshape(1, C2), second_shift.reshape(1, C2))

time: 33.4 us -> 32.6 us (0.976)
  Pallas kernels: 33.2 us -> 32.4 us
    pallas_call x1, Pallas kernels: 27.2 us -> 26.2 us  [per_device(): pl.pallas_call(kernel, out_shape=jax.ShapeDtypeStruct((2, (TR + 2) * PITC...]
where the time goes in v4:
time: 32.6 us; the launch traced here: 32.4 us
  Pallas kernels  32.4 us (99%)
    pallas_call x1, Pallas kernels, per_device(): pl.pallas_call(kernel, out_shape=jax.ShapeDtypeStruct((2, (TR + 2) * PITC...  26.2 us
    pallas_call x1, Pallas kernels, per_device(): pl.pallas_call(second_kernel, out_shape=jax.ShapeDtypeStruct((TR, TW, C2)...  6.18 us

profile of v4, /device:TPU:1, one launch (start us, length us, event | category | flops | bytes accessed | tf_op | source)
XLA Modules:
  0.0 32.4 jit_solution(8936200420385139547)
XLA Ops:
  0.0 0.0 copy-start
  0.0 0.0 copy-start.1
  0.0 0.0 copy-start.2
  0.0 26.2 %shard_map.127.h32 = f32[2,5200,128]{2,1,0:T(8,128)S(1)} custom-call(bf16[256,384]{1,0:T(8,128)(2,1)} %bitcast.12, s32[1,64]{1,0:T(1,128)} %bitcast.15, s32[1,64]{1,0:T(1,128)} %bitcast.16, s32[1,64]{1,0:T(1,128)} %bitcast.17, s32[1,128]{1,0:T(1,128)} %bitcast.18, bf16[54,128]{1,0:T(8,128)(2,1)} %stem_w_h.1, f32[1,128]{1,0:T(1,128)} %bitcast.19, ...), custom_call_target="tpu_custom_call" | custom-call | flops 2700000000 | bytes 2000000 | tf_op jit(solution)/shard_map/pallas_call | solution.py:346
  26.2 0.0 copy-done
  26.2 0.0 copy-done.1
  26.2 0.0 copy-done.2
  26.2 6.2 %shard_map.128 = bf16[128,32,256]{2,1,0:T(8,128)(2,1)} custom-call(f32[2,5200,128]{2,1,0:T(8,128)S(1)} %shard_map.127.h32, bf16[2304,256]{1,0:T(8,128)(2,1)S(1)} %copy-done, f32[1,256]{1,0:T(1,128)S(1)} %bitcast.10, f32[1,256]{1,0:T(1,128)S(1)} %bitcast.11), custom_call_target="tpu_custom_call" | custom-call | flops 4800000000 | bytes 3000000 | tf_op jit(solution)/shard_map/pallas_call | solution.py:357
Async XLA Ops:
  0.0 26.2 %copy-start = (bf16[2304,256]{1,0:T(8,128)(2,1)S(1)}, bf16[2304,256]{1,0:T(8,128)(2,1)}, u32[]{:S(2)}) copy-start(bf16[2304,256]{1,0:T(8,128)(2,1)} %w2.1) | copy-start | bytes 3538948
  0.0 26.2 %copy-start.1 = (f32[256]{0:T(256)S(1)}, f32[256]{0:T(256)}, u32[]{:S(2)}) copy-start(f32[256]{0:T(256)} %param.24) | copy-start | bytes 3076
  0.0 26.2 %copy-start.2 = (f32[256]{0:T(256)S(1)}, f32[256]{0:T(256)}, u32[]{:S(2)}) copy-start(f32[256]{0:T(256)} %param.25) | copy-start | bytes 3076

commit v5 on v4

--- a/solution.py
+++ b/solution.py
@@ -12,7 +12,7 @@
 C1, C2 = 128, 256
 PITCH1 = 152
 PITCH2 = 40
-MID = 112
+MID = 128
 CB = 15
 PARTS = (32, 32, 32, 32)
 BF, F32 = jnp.bfloat16, jnp.float32
@@ -194,20 +194,17 @@
         halo.append((copy, sends, receives))
     def lay_middle(t):
         for a in range(3):
-            start = pl.multiple_of(t * PITCH1, 8) + 22 + a
+            start = pl.multiple_of(t * PITCH1, 8) + 7 + a
             middle[t, :, 128 * a : 128 * a + 128] = b32[pl.ds(start, MID), :].astype(BF)
 
-    def lay_ends(t):
-        for a in range(3):
-            for n in range(2):
-                start = pl.multiple_of(t * PITCH1, 8) + 6 + a + 128 * n
-                ends[t, 16 * n : 16 * n + 16, 128 * a : 128 * a + 128] = b32[pl.ds(start, 16), :].astype(BF)
+    def finish_first(pixels):
+        summed = jnp.dot(pixels, w1[...], preferred_element_type=F32)
+        return jnp.maximum(summed * scale1[...] + shift1[...], 0.0).astype(BF).astype(F32)
 
     def first_conv(source, t, columns):
         height = source.shape[1]
         pixels = [source[pl.ds(t + b, columns)].reshape(columns * height, 3 * C1) for b in range(3)]
-        summed = jnp.dot(jnp.concatenate(pixels, axis=1), w1[...], preferred_element_type=F32)
-        value = jnp.maximum(summed * scale1[...] + shift1[...], 0.0).astype(BF).astype(F32)
+        value = finish_first(jnp.concatenate(pixels, axis=1))
         return value.reshape(columns, height, C2)
 
     def loop(start, stop, step, unroll):
@@ -226,7 +223,7 @@
         value = first_conv(middle, t, CB)
         for m in range(CB):
             for c in range(2):
-                h32[c, pl.ds(16 * PITCH2 + t + m, MID, stride=PITCH2), :] = value[m, :, 128 * c : 128 * c + 128]
+                h32[c, pl.ds(PITCH2 + t + m, MID, stride=PITCH2), :] = value[m, :, 128 * c : 128 * c + 128]
 
     loop(0, (TW - 2) // CB, middle_block, 1)
 
@@ -254,31 +251,32 @@
                 at = column * PITCH1 + 6 + r + (TR + 2 if lower else 0)
                 b32[at : at + 1] = values[picked : picked + 1]
 
-    loop(0, TW + 4, lay_ends, 4)
     for t in (0, 1, TW + 2, TW + 3):
         lay_middle(t)
 
-    for t, inside in ((0, has_left), (TW, has_right)):
-        value = first_conv(middle, t, 2)
-        for m in range(2):
-            kept = value[m]
-            if t + m in (0, TW + 1):
-                kept = jnp.where(inside, kept, 0.0)
-            for c in range(2):
-                h32[c, pl.ds(16 * PITCH2 + t + m, MID, stride=PITCH2), :] = kept[:, 128 * c : 128 * c + 128]
-
-    rows = iota((32, C2), 0)
-    keep_rows = ((rows > 0) | has_up) & ((rows < 17) | has_down)
-    value = first_conv(ends, 0, TW + 2)
-    for t in range(TW + 2):
-        keep = keep_rows
+    for n, h in enumerate((0, 1, TR, TR + 1)):
+        for b in range(3):
+            for a in range(3):
+                line = b32[pl.ds(b * PITCH1 + 6 + h + a, TW + 2, stride=PITCH1), :]
+                lanes = 128 * (3 * b + a)
+                ends[n, : TW + 2, lanes : lanes + 128] = line.astype(BF)
+    pixels = [
+        jnp.concatenate([middle[pl.ds(t + b, 2)].reshape(2 * MID, 3 * C1) for b in range(3)], axis=1) for t in (0, TW)
+    ]
+    both = finish_first(jnp.concatenate(pixels + [ends[...].reshape(4 * 48, 9 * C1)], axis=0))
+    for n, (t, inside) in enumerate(((0, has_left), (1, True), (TW, True), (TW + 1, has_right))):
+        kept = both[MID * n : MID * n + MID]
         if t in (0, TW + 1):
-            keep = keep & (has_right if t else has_left)
-        kept = jnp.where(keep, value[t], 0.0)
+            kept = jnp.where(inside, kept, 0.0)
         for c in range(2):
-            lanes = slice(128 * c, 128 * c + 128)
-            h32[c, pl.ds(t, 16, stride=PITCH2), :] = kept[:16, lanes]
-            h32[c, pl.ds(128 * PITCH2 + t, 2, stride=PITCH2), :] = kept[16:18, lanes]
+            h32[c, pl.ds(PITCH2 + t, MID, stride=PITCH2), :] = kept[:, 128 * c : 128 * c + 128]
+    value = both[4 * MID :].reshape(4, 48, C2)
+    columns = iota((48, C2), 0)
+    keep_columns = ((columns > 0) | has_left) & ((columns < TW + 1) | has_right)
+    for n, (h, inside) in enumerate(((0, has_up), (1, True), (TR, True), (TR + 1, has_down))):
+        kept = jnp.where(keep_columns & inside, value[n], 0.0)
+        for c in range(2):
+            h32[c, h * PITCH2 : h * PITCH2 + TW + 2] = kept[: TW + 2, 128 * c : 128 * c + 128]
 
     exchange.wait_send()
     for copy, sends, _ in halo:
@@ -340,7 +338,7 @@
         v((DEV * 16, 128), F32), v((384, 1024), F32), v((384, 1024), BF),
         v(((TW + 4) * PITCH1, 128), F32), v((4, TR, 128), BF), v((2, 2, TW, 128), BF),
         v((2, 2, TR, 128), BF), v((2, 2, TW, 128), BF), v((4, 2, TW // 2, 128), BF),
-        v((TW + 4, MID, 384), BF), v((TW + 4, 32, 384), BF),
+        v((TW + 4, MID, 384), BF), v((4, 48, 9 * C1), BF),
         dma, dma((8,)), dma((9,)), dma, dma, dma((8,)), dma((8,)),
     ]
     hidden = pl.pallas_call(

time: 32.6 us -> 32.2 us (0.988)
  Pallas kernels: 32.4 us -> 32 us
    pallas_call x1, Pallas kernels: 26.2 us -> 25.8 us  [per_device(): pl.pallas_call(kernel, out_shape=jax.ShapeDtypeStruct((2, (TR + 2) * PITC...]
where the time goes in v5:
time: 32.2 us; the launch traced here: 32.1 us
  Pallas kernels  32 us (99%)
    pallas_call x1, Pallas kernels, per_device(): pl.pallas_call(kernel, out_shape=jax.ShapeDtypeStruct((2, (TR + 2) * PITC...  25.8 us
    pallas_call x1, Pallas kernels, per_device(): pl.pallas_call(second_kernel, out_shape=jax.ShapeDtypeStruct((TR, TW, C2)...  6.18 us

profile of v5, /device:TPU:1, one launch (start us, length us, event | category | flops | bytes accessed | tf_op | source)
XLA Modules:
  0.0 32.1 jit_solution(13587342272416230042)
XLA Ops:
  0.0 0.0 copy-start
  0.0 0.0 copy-start.1
  0.0 0.0 copy-start.2
  0.0 25.8 %shard_map.127.h32 = f32[2,5200,128]{2,1,0:T(8,128)S(1)} custom-call(bf16[256,384]{1,0:T(8,128)(2,1)} %bitcast.12, s32[1,64]{1,0:T(1,128)} %bitcast.15, s32[1,64]{1,0:T(1,128)} %bitcast.16, s32[1,64]{1,0:T(1,128)} %bitcast.17, s32[1,128]{1,0:T(1,128)} %bitcast.18, bf16[54,128]{1,0:T(8,128)(2,1)} %stem_w_h.1, f32[1,128]{1,0:T(1,128)} %bitcast.19, ...), custom_call_target="tpu_custom_call" | custom-call | flops 2700000000 | bytes 2000000 | tf_op jit(solution)/shard_map/pallas_call | solution.py:344
  25.8 0.0 copy-done
  25.9 0.0 copy-done.1
  25.9 0.0 copy-done.2
  25.9 6.2 %shard_map.128 = bf16[128,32,256]{2,1,0:T(8,128)(2,1)} custom-call(f32[2,5200,128]{2,1,0:T(8,128)S(1)} %shard_map.127.h32, bf16[2304,256]{1,0:T(8,128)(2,1)S(1)} %copy-done, f32[1,256]{1,0:T(1,128)S(1)} %bitcast.10, f32[1,256]{1,0:T(1,128)S(1)} %bitcast.11), custom_call_target="tpu_custom_call" | custom-call | flops 4800000000 | bytes 3000000 | tf_op jit(solution)/shard_map/pallas_call | solution.py:355
Async XLA Ops:
  0.0 25.9 %copy-start = (bf16[2304,256]{1,0:T(8,128)(2,1)S(1)}, bf16[2304,256]{1,0:T(8,128)(2,1)}, u32[]{:S(2)}) copy-start(bf16[2304,256]{1,0:T(8,128)(2,1)} %w2.1) | copy-start | bytes 3538948
  0.0 25.9 %copy-start.1 = (f32[256]{0:T(256)S(1)}, f32[256]{0:T(256)}, u32[]{:S(2)}) copy-start(f32[256]{0:T(256)} %param.24) | copy-start | bytes 3076
  0.0 25.9 %copy-start.2 = (f32[256]{0:T(256)S(1)}, f32[256]{0:T(256)}, u32[]{:S(2)}) copy-start(f32[256]{0:T(256)} %param.25) | copy-start | bytes 3076

commit v6 on v5

--- a/solution.py
+++ b/solution.py
@@ -13,7 +13,7 @@
 PITCH1 = 152
 PITCH2 = 40
 MID = 128
-CB = 15
+CB = 5
 PARTS = (32, 32, 32, 32)
 BF, F32 = jnp.bfloat16, jnp.float32
 MESH = pl.DeviceIdType.MESH
@@ -194,8 +194,8 @@
         halo.append((copy, sends, receives))
     def lay_middle(t):
         for a in range(3):
-            start = pl.multiple_of(t * PITCH1, 8) + 7 + a
-            middle[t, :, 128 * a : 128 * a + 128] = b32[pl.ds(start, MID), :].astype(BF)
+            start = t * PITCH1 + 7 + a
+            middle[t, :, 128 * a : 128 * a + 128] = b32[start : start + MID].astype(BF)
 
     def finish_first(pixels):
         summed = jnp.dot(pixels, w1[...], preferred_element_type=F32)
@@ -203,29 +203,22 @@
 
     def first_conv(source, t, columns):
         height = source.shape[1]
-        pixels = [source[pl.ds(t + b, columns)].reshape(columns * height, 3 * C1) for b in range(3)]
+        pixels = [source[t + b : t + b + columns].reshape(columns * height, 3 * C1) for b in range(3)]
         value = finish_first(jnp.concatenate(pixels, axis=1))
         return value.reshape(columns, height, C2)
 
-    def loop(start, stop, step, unroll):
-        def body(n, carry):
-            step(n)
-            return carry
-
-        lax.fori_loop(start, stop, body, 0, unroll=unroll)
-
-    loop(2, TW + 2, lay_middle, 5)
     for copy in weight_loads:
         copy.wait()
 
-    def middle_block(n):
-        t = 2 + n * CB
+    laid = 2
+    for t in range(2, TW, CB):
+        for column in range(laid, t + CB + 2):
+            lay_middle(column)
+        laid = t + CB + 2
         value = first_conv(middle, t, CB)
         for m in range(CB):
             for c in range(2):
                 h32[c, pl.ds(PITCH2 + t + m, MID, stride=PITCH2), :] = value[m, :, 128 * c : 128 * c + 128]
-
-    loop(0, (TW - 2) // CB, middle_block, 1)
 
     for copy, _, receives in halo:
         pl.when(receives)(copy.wait_recv)

time: 32.2 us -> 31.8 us (0.988)
  Pallas kernels: 32 us -> 31.6 us
    pallas_call x1, Pallas kernels: 25.8 us -> 25.4 us  [per_device(): pl.pallas_call(kernel, out_shape=jax.ShapeDtypeStruct((2, (TR + 2) * PITC...]
where the time goes in v6:
time: 31.8 us; the launch traced here: 31.7 us
  Pallas kernels  31.6 us (99%)
    pallas_call x1, Pallas kernels, per_device(): pl.pallas_call(kernel, out_shape=jax.ShapeDtypeStruct((2, (TR + 2) * PITC...  25.4 us
    pallas_call x1, Pallas kernels, per_device(): pl.pallas_call(second_kernel, out_shape=jax.ShapeDtypeStruct((TR, TW, C2)...  6.2 us

profile of v6, /device:TPU:1, one launch (start us, length us, event | category | flops | bytes accessed | tf_op | source)
XLA Modules:
  0.0 31.7 jit_solution(5509081104411067311)
XLA Ops:
  0.0 0.0 copy-start
  0.0 0.0 copy-start.1
  0.0 0.0 copy-start.2
  0.0 25.4 %shard_map.127.h32 = f32[2,5200,128]{2,1,0:T(8,128)S(1)} custom-call(bf16[256,384]{1,0:T(8,128)(2,1)} %bitcast.12, s32[1,64]{1,0:T(1,128)} %bitcast.15, s32[1,64]{1,0:T(1,128)} %bitcast.16, s32[1,64]{1,0:T(1,128)} %bitcast.17, s32[1,128]{1,0:T(1,128)} %bitcast.18, bf16[54,128]{1,0:T(8,128)(2,1)} %stem_w_h.1, f32[1,128]{1,0:T(1,128)} %bitcast.19, ...), custom_call_target="tpu_custom_call" | custom-call | flops 2700000000 | bytes 2000000 | tf_op jit(solution)/shard_map/pallas_call | solution.py:337
  25.5 0.0 copy-done
  25.5 0.0 copy-done.1
  25.5 0.0 copy-done.2
  25.5 6.2 %shard_map.128 = bf16[128,32,256]{2,1,0:T(8,128)(2,1)} custom-call(f32[2,5200,128]{2,1,0:T(8,128)S(1)} %shard_map.127.h32, bf16[2304,256]{1,0:T(8,128)(2,1)S(1)} %copy-done, f32[1,256]{1,0:T(1,128)S(1)} %bitcast.10, f32[1,256]{1,0:T(1,128)S(1)} %bitcast.11), custom_call_target="tpu_custom_call" | custom-call | flops 4800000000 | bytes 3000000 | tf_op jit(solution)/shard_map/pallas_call | solution.py:348
Async XLA Ops:
  0.0 25.5 %copy-start = (bf16[2304,256]{1,0:T(8,128)(2,1)S(1)}, bf16[2304,256]{1,0:T(8,128)(2,1)}, u32[]{:S(2)}) copy-start(bf16[2304,256]{1,0:T(8,128)(2,1)} %w2.1) | copy-start | bytes 3538948
  0.0 25.5 %copy-start.1 = (f32[256]{0:T(256)S(1)}, f32[256]{0:T(256)}, u32[]{:S(2)}) copy-start(f32[256]{0:T(256)} %param.24) | copy-start | bytes 3076
  0.0 25.5 %copy-start.2 = (f32[256]{0:T(256)S(1)}, f32[256]{0:T(256)}, u32[]{:S(2)}) copy-start(f32[256]{0:T(256)} %param.25) | copy-start | bytes 3076
